TPU v7x, 32 devices: a whole 2x2x4 slice. The times are simulated.
32 devices in a mesh: groups: 2 (over y), cluster: 8 (over z, x), inner: 2 (over core).
Axes of the slice: x: 2, y: 2, z: 4, core: 2. Of those that a mesh axis runs over, the one named last changes fastest.
Arguments:
- right_sides: float32 [64, 65536], P(None, ('groups', 'cluster', 'inner')), parts along dimension 1, may hold values from -6 to 6
- tree_order: int32 [16, 2048], P(('cluster', 'inner')), may hold values from 0 to 2047, each once within a row
- leaf_inverse: float32 [128, 256, 256], P(('cluster', 'inner')), may hold values from -0.375 to 0.375
- reduce_low: float32 [128, 32768], P(None, ('cluster', 'inner')), may hold values from -0.09375 to 0.09375
- expand_low: float32 [128, 32768], P(None, ('cluster', 'inner')), may hold values from -0.5 to 0.5
- reduce_mid: float32 [128, 32768], P(None, ('cluster', 'inner')), may hold values from -0.0625 to 0.0625
- expand_mid: float32 [128, 32768], P(None, ('cluster', 'inner')), may hold values from -0.5 to 0.5
- reduce_top: float32 [128, 32768], P(None, ('cluster', 'inner')), may hold values from -0.046875 to 0.046875
- expand_top: float32 [128, 32768], P(None, ('cluster', 'inner')), may hold values from -0.5 to 0.5
- coupling_low: float32 [4, 256, 256], replicated, may hold values from -0.375 to 0.375
- coupling_mid: float32 [2, 256, 256], replicated, may hold values from -0.375 to 0.375
- coupling_top: float32 [1, 256, 256], replicated, may hold values from -0.375 to 0.375
Outputs:
- solution: float32 [64, 65536], P(None, ('groups', 'cluster', 'inner')), parts along dimension 1
There are 2 independent parts, one for each index of `groups`. A program takes and returns all parts, laid end to end along the dimension named above; an argument that names none is the same for every part. Nothing has to cross between parts.
Inputs may be any that keep to these rules, and one draw needn't show every extreme that they name: Each row of tree_order is a permutation of 0 to 2047.
All inputs are finite; a program needn't handle non-finite values.
Results may differ from a plain program's by a relative error of at most 0.000082.
Values sent between devices are 32-bit elements; how exact they have to be, the bound alone decides.
A program may use at most 64 MiB of HBM per device.

v0:
```python
import jax
import jax.numpy as jnp
from jax import lax
from jax.sharding import PartitionSpec as P

HIGH = lax.Precision.HIGHEST


def partner(shard, axis, bit):
    return lax.ppermute(shard, axis, [(i, i ^ 1 << bit) for i in range(lax.axis_size(axis))])


def apply_level(field, reduce_basis, expand_basis, coupling, level):
    rank = reduce_basis.shape[0]
    rhs_count = field.shape[0]
    partial_value = lax.dot_general(
        field,
        reduce_basis,
        (((1,), (1,)), ((), ())),
        precision=HIGH,
        preferred_element_type=jnp.float32,
    )
    partial_value = lax.psum(partial_value, "inner")
    cluster_bits = lax.axis_size("cluster").bit_length() - 1
    shift_bits = cluster_bits - level
    position = lax.axis_index("cluster")
    child_bit = position >> shift_bits & 1
    node_index = position >> shift_bits + 1
    running = partial_value
    for bit_pos in range(shift_bits):
        running = running + partner(running, "cluster", bit_pos)
    other_sum = partner(running, "cluster", shift_bits)
    paired = jnp.where(
        child_bit == 0, jnp.stack([running, other_sum]), jnp.stack([other_sum, running])
    )
    stacked = paired.transpose(1, 0, 2).reshape(rhs_count, 2 * rank)
    node_matrix = lax.dynamic_index_in_dim(coupling, node_index, 0, keepdims=False)
    solved = lax.dot_general(
        stacked,
        node_matrix,
        (((1,), (1,)), ((), ())),
        precision=HIGH,
        preferred_element_type=jnp.float32,
    )
    own_half = lax.dynamic_slice_in_dim(solved, child_bit * rank, rank, 1)
    return field - jnp.dot(
        own_half, expand_basis, precision=HIGH, preferred_element_type=jnp.float32
    )


def on_device(
    right_sides,
    tree_order,
    leaf_inverse,
    reduce_low,
    expand_low,
    reduce_mid,
    expand_mid,
    reduce_top,
    expand_top,
    coupling_low,
    coupling_mid,
    coupling_top,
):
    rhs_count = right_sides.shape[0]
    local_order = tree_order[0]
    ordered = jnp.take(right_sides, local_order, axis=1)
    leaf_size = leaf_inverse.shape[1]
    pieces = ordered.reshape(rhs_count, -1, leaf_size)
    field = jnp.einsum("rbl,bkl->rbk", pieces, leaf_inverse, precision=HIGH).reshape(rhs_count, -1)
    field = apply_level(field, reduce_low, expand_low, coupling_low, 3)
    field = apply_level(field, reduce_mid, expand_mid, coupling_mid, 2)
    field = apply_level(field, reduce_top, expand_top, coupling_top, 1)
    return jnp.zeros_like(field).at[:, local_order].set(field)


def solution(mesh):
    in_specs = (
        P(None, ("groups", "cluster", "inner")),
        P(("cluster", "inner"), None),
        P(("cluster", "inner"), None, None),
        P(None, ("cluster", "inner")),
        P(None, ("cluster", "inner")),
        P(None, ("cluster", "inner")),
        P(None, ("cluster", "inner")),
        P(None, ("cluster", "inner")),
        P(None, ("cluster", "inner")),
        P(),
        P(),
        P(),
    )
    out_specs = P(None, ("groups", "cluster", "inner"))
    return jax.shard_map(
        on_device, mesh=mesh, in_specs=in_specs, out_specs=out_specs, check_vma=False
    )
```

profile of v0, /device:TPU:0, one launch (start us, length us, event | category | flops | bytes accessed | tf_op | source)
XLA Modules:
  0.0 71.8 jit_solution(17639844889611444592)
XLA Ops:
  0.0 0.0 copy-start
  0.0 0.9 %compare_select_fusion = s32[2048,1]{0,1:T(1,128)S(1)} fusion(s32[1,2048]{1,0:T(1,128)} %param.13), kind=kLoop, calls=%fused_computation.32 | loop fusion | flops 6144 | bytes 16384 | tf_op jit(solution)/shard_map/select_n | solution.py:74
  0.9 1.4 %copy.17 = f32[64,2048]{0,1:T(8,128)S(1)} copy(f32[64,2048]{1,0:T(8,128)} %param.12) | data formatting | bytes 1048576 | tf_op args[0]
  2.3 0.0 copy-start.5
  2.3 7.6 %gather_fusion = f32[2048,64]{1,0:T(8,128)} fusion(f32[64,2048]{0,1:T(8,128)S(1)} %copy.17, s32[2048]{0:T(1024)S(1)} %broadcast_clamp_fusion), kind=kCustom, calls=%fused_computation | custom fusion | bytes 1056768 | tf_op jit(solution)/shard_map/jit(_take)/gather | solution.py:67
  9.8 1.5 %copy.18 = f32[64,8,256]{2,0,1:T(8,128)S(1)} copy(f32[64,8,256]{0,2,1:T(8,128)} %bitcast.63) | data formatting | bytes 1048576 | tf_op jit(solution)/shard_map/jit(_take)/gather | solution.py:67
  11.4 0.5 broadcast.38
  11.9 0.0 copy-done.5
  11.9 0.7 reduce.3
  12.6 0.0 copy-done
  12.6 0.0 copy-start.1
  12.6 2.0 %convolution_bitcast_fusion = f32[8,8,8,256]{3,2,1,0:T(8,128)S(1)} fusion(f32[8,256,256]{2,1,0:T(8,128)S(1)} %copy-done, f32[64,8,256]{2,0,1:T(8,128)S(1)} %copy.18, pred[8,256]{1,0:T(8,128)(4,1)S(1)} %compare_and_fusion), kind=kOutput, calls=%fused_computation.6 | convolution fusion | flops 402784256 | bytes 3147776 | tf_op jit(solution)/shard_map/rbl,bkl->rbk/dot_general | solution.py:70
  14.7 0.0 copy-done.1
  14.7 1.2 %fusion.32 = f32[64,128]{1,0:T(8,128)S(1)} fusion(f32[64,2048]{1,0:T(8,128)S(1)} %bitcast.61, f32[128,2048]{1,0:T(8,128)S(1)} %copy-done.1), kind=kOutput, calls=%fused_computation.45 | convolution fusion | flops 201326592 | bytes 1605632 | tf_op jit(solution)/shard_map/dot_general | solution.py:16
  15.9 3.7 %psum.21 = f32[64,128]{1,0:T(8,128)S(1)} all-reduce(f32[64,128]{1,0:T(8,128)S(1)} %fusion.32), channel_id=1, replica_groups=mesh['groups'=2,'cluster'=8,'inner'=2] {'inner'}, use_global_device_ids=true, to_apply=%region_0.1 | all-reduce | flops 8192 | bytes 65536 | tf_op jit(solution)/shard_map/psum | solution.py:23
  19.6 2.7 %collective-permute-start = (f32[64,128]{1,0:T(8,128)S(1)}, f32[64,128]{1,0:T(8,128)S(1)}, u32[]{:S(2)}, u32[]{:S(2)}) collective-permute-start(f32[64,128]{1,0:T(8,128)S(1)} %psum.21), channel_id=1, source_target_pairs={{0,2},{2,0},{4,6},{6,4},{8,10},{10,8},{12,14},{14,12},{1,3},{3,1},... | collective-permute-start | bytes 98312 | tf_op jit(solution)/shard_map/ppermute | solution.py:10
  22.3 0.0 copy-start.2
  22.3 1.9 %collective-permute-done = f32[64,128]{1,0:T(8,128)S(1)} collective-permute-done((f32[64,128]{1,0:T(8,128)S(1)}, f32[64,128]{1,0:T(8,128)S(1)}, u32[]{:S(2)}, u32[]{:S(2)}) %collective-permute-start) | collective-permute-done | bytes 32800 | tf_op jit(solution)/shard_map/ppermute | solution.py:10
  24.2 1.3 %fusion.8 = f32[64,256]{1,0:T(8,128)S(1)} fusion(f32[4,256,256]{2,1,0:T(8,128)} %param.21, s32[]{:T(128)S(6)} %select_n.67, f32[1,64,128]{2,1,0:T(8,128)S(1)} %bitcast.67, f32[1,64,128]{2,1,0:T(8,128)S(1)} %bitcast.66, pred[]{:T(512)S(6)} %eq.9), kind=kOutput, calls=%fused_computation.14 | convolution fusion | flops 50380800 | bytes 393221 | tf_op jit(solution)/shard_map/dot_general | solution.py:38
  25.5 1.9 %convolution_subtract_fusion.2 = f32[64,2048]{1,0:T(8,128)S(1)} fusion(f32[64,2048]{1,0:T(8,128)S(1)} %bitcast.62, f32[128,2048]{1,0:T(8,128)} %param.16, f32[64,256]{1,0:T(8,128)S(1)} %fusion.8, s32[]{:T(128)S(6)} %select_n.68), kind=kOutput, calls=%fused_computation.4 | convolution fusion | flops 201457664 | bytes 2129924 | tf_op jit(solution)/shard_map/dot_general | solution.py:46
  27.5 0.0 copy-done.2
  27.5 1.2 %fusion.33 = f32[64,128]{1,0:T(8,128)S(1)} fusion(f32[64,2048]{1,0:T(8,128)S(1)} %convolution_subtract_fusion.2, f32[128,2048]{1,0:T(8,128)S(1)} %copy-done.2), kind=kOutput, calls=%fused_computation.46 | convolution fusion | flops 201326592 | bytes 1605632 | tf_op jit(solution)/shard_map/dot_general | solution.py:16
  28.7 3.4 %psum.22 = f32[64,128]{1,0:T(8,128)S(1)} all-reduce(f32[64,128]{1,0:T(8,128)S(1)} %fusion.33), channel_id=1, replica_groups=mesh['groups'=2,'cluster'=8,'inner'=2] {'inner'}, use_global_device_ids=true, to_apply=%region_1.2 | all-reduce | flops 8192 | bytes 65536 | tf_op jit(solution)/shard_map/psum | solution.py:23
  32.1 2.1 %collective-permute-start.1 = (f32[64,128]{1,0:T(8,128)S(1)}, f32[64,128]{1,0:T(8,128)S(1)}, u32[]{:S(2)}, u32[]{:S(2)}) collective-permute-start(f32[64,128]{1,0:T(8,128)S(1)} %psum.22), channel_id=1, source_target_pairs={{0,2},{2,0},{4,6},{6,4},{8,10},{10,8},{12,14},{14,12},{1,3},{3,1},... | collective-permute-start | bytes 98312 | tf_op jit(solution)/shard_map/ppermute | solution.py:10
  34.2 1.9 %collective-permute-done.1 = f32[64,128]{1,0:T(8,128)S(1)} collective-permute-done((f32[64,128]{1,0:T(8,128)S(1)}, f32[64,128]{1,0:T(8,128)S(1)}, u32[]{:S(2)}, u32[]{:S(2)}) %collective-permute-start.1) | collective-permute-done | bytes 32800 | tf_op jit(solution)/shard_map/ppermute | solution.py:10
  36.1 2.1 %collective-permute-start.2 = (f32[64,128]{1,0:T(8,128)S(1)}, f32[64,128]{1,0:T(8,128)S(1)}, u32[]{:S(2)}, u32[]{:S(2)}) collective-permute-start(f32[64,128]{1,0:T(8,128)S(1)} %add.64), channel_id=1, source_target_pairs={{0,4},{2,6},{4,0},{6,2},{8,12},{10,14},{12,8},{14,10},{1,5},{3,7},... | collective-permute-start | bytes 98312 | tf_op jit(solution)/shard_map/ppermute | solution.py:10
  38.2 0.0 copy-start.3
  38.2 1.9 %collective-permute-done.2 = f32[64,128]{1,0:T(8,128)S(1)} collective-permute-done((f32[64,128]{1,0:T(8,128)S(1)}, f32[64,128]{1,0:T(8,128)S(1)}, u32[]{:S(2)}, u32[]{:S(2)}) %collective-permute-start.2) | collective-permute-done | bytes 32800 | tf_op jit(solution)/shard_map/ppermute | solution.py:10
  40.1 1.3 %fusion.6 = f32[64,256]{1,0:T(8,128)S(1)} fusion(f32[2,256,256]{2,1,0:T(8,128)} %param.22, s32[]{:T(128)S(6)} %select_n.71, f32[1,64,128]{2,1,0:T(8,128)S(1)} %bitcast.68, f32[1,64,128]{2,1,0:T(8,128)S(1)} %bitcast.64, pred[]{:T(512)S(6)} %eq.10), kind=kOutput, calls=%fused_computation.12 | convolution fusion | flops 50380800 | bytes 393221 | tf_op jit(solution)/shard_map/dot_general | solution.py:38
  41.4 0.0 copy-start.4
  41.4 2.0 %convolution_subtract_fusion.1 = f32[64,2048]{1,0:T(8,128)S(1)} fusion(f32[64,2048]{1,0:T(8,128)S(1)} %convolution_subtract_fusion.2, f32[128,2048]{1,0:T(8,128)} %param.18, f32[64,256]{1,0:T(8,128)S(1)} %fusion.6, s32[]{:T(128)S(6)} %select_n.72), kind=kOutput, calls=%fused_computation.3 | convolution fusion | flops 201457664 | bytes 2129924 | tf_op jit(solution)/shard_map/dot_general | solution.py:46
  43.4 0.0 copy-done.3
  43.4 1.2 %fusion.34 = f32[64,128]{1,0:T(8,128)S(1)} fusion(f32[64,2048]{1,0:T(8,128)S(1)} %convolution_subtract_fusion.1, f32[128,2048]{1,0:T(8,128)S(1)} %copy-done.3), kind=kOutput, calls=%fused_computation.47 | convolution fusion | flops 201326592 | bytes 1605632 | tf_op jit(solution)/shard_map/dot_general | solution.py:16
  44.6 3.4 %psum.23 = f32[64,128]{1,0:T(8,128)S(1)} all-reduce(f32[64,128]{1,0:T(8,128)S(1)} %fusion.34), channel_id=1, replica_groups=mesh['groups'=2,'cluster'=8,'inner'=2] {'inner'}, use_global_device_ids=true, to_apply=%region_2.3 | all-reduce | flops 8192 | bytes 65536 | tf_op jit(solution)/shard_map/psum | solution.py:23
  48.0 2.0 %collective-permute-start.3 = (f32[64,128]{1,0:T(8,128)S(1)}, f32[64,128]{1,0:T(8,128)S(1)}, u32[]{:S(2)}, u32[]{:S(2)}) collective-permute-start(f32[64,128]{1,0:T(8,128)S(1)} %psum.23), channel_id=1, source_target_pairs={{0,2},{2,0},{4,6},{6,4},{8,10},{10,8},{12,14},{14,12},{1,3},{3,1},... | collective-permute-start | bytes 98312 | tf_op jit(solution)/shard_map/ppermute | solution.py:10
  50.0 2.0 %collective-permute-done.3 = f32[64,128]{1,0:T(8,128)S(1)} collective-permute-done((f32[64,128]{1,0:T(8,128)S(1)}, f32[64,128]{1,0:T(8,128)S(1)}, u32[]{:S(2)}, u32[]{:S(2)}) %collective-permute-start.3) | collective-permute-done | bytes 32800 | tf_op jit(solution)/shard_map/ppermute | solution.py:10
  52.0 2.0 %collective-permute-start.4 = (f32[64,128]{1,0:T(8,128)S(1)}, f32[64,128]{1,0:T(8,128)S(1)}, u32[]{:S(2)}, u32[]{:S(2)}) collective-permute-start(f32[64,128]{1,0:T(8,128)S(1)} %add.67), channel_id=1, source_target_pairs={{0,4},{2,6},{4,0},{6,2},{8,12},{10,14},{12,8},{14,10},{1,5},{3,7},... | collective-permute-start | bytes 98312 | tf_op jit(solution)/shard_map/ppermute | solution.py:10
  54.0 1.9 %collective-permute-done.4 = f32[64,128]{1,0:T(8,128)S(1)} collective-permute-done((f32[64,128]{1,0:T(8,128)S(1)}, f32[64,128]{1,0:T(8,128)S(1)}, u32[]{:S(2)}, u32[]{:S(2)}) %collective-permute-start.4) | collective-permute-done | bytes 32800 | tf_op jit(solution)/shard_map/ppermute | solution.py:10
  55.9 3.0 %collective-permute-start.5 = (f32[64,128]{1,0:T(8,128)S(1)}, f32[64,128]{1,0:T(8,128)S(1)}, u32[]{:S(2)}, u32[]{:S(2)}) collective-permute-start(f32[64,128]{1,0:T(8,128)S(1)} %add.68), channel_id=1, source_target_pairs={{0,8},{2,10},{4,12},{6,14},{8,0},{10,2},{12,4},{14,6},{1,9},{3,11}... | collective-permute-start | bytes 98312 | tf_op jit(solution)/shard_map/ppermute | solution.py:10
  59.0 1.9 %collective-permute-done.5 = f32[64,128]{1,0:T(8,128)S(1)} collective-permute-done((f32[64,128]{1,0:T(8,128)S(1)}, f32[64,128]{1,0:T(8,128)S(1)}, u32[]{:S(2)}, u32[]{:S(2)}) %collective-permute-start.5) | collective-permute-done | bytes 32800 | tf_op jit(solution)/shard_map/ppermute | solution.py:10
  60.8 0.0 copy-done.4
  60.9 0.4 fusion.4
  61.2 1.9 %fusion = f32[2048,64]{0,1:T(8,128)S(1)} fusion(f32[64,2048]{1,0:T(8,128)S(1)} %convolution_subtract_fusion.1, f32[128,2048]{1,0:T(8,128)} %param.20, f32[64,256]{1,0:T(8,128)S(1)} %fusion.4, s32[]{:T(128)S(6)} %select_n.75), kind=kOutput, calls=%fused_computation.5 | convolution fusion | flops 201457664 | bytes 2129924 | tf_op jit(solution)/shard_map/dot_general | solution.py:46
  63.1 1.3 %copy.23 = f32[2048,64]{1,0:T(8,128)} copy(f32[2048,64]{0,1:T(8,128)S(1)} %fusion) | data formatting | bytes 1048576 | tf_op jit(solution)/shard_map/sub | solution.py:46
  64.5 6.2 %scatter_custom_fusion = f32[64,2048]{0,1:T(8,128)S(1)} fusion(s32[2048]{0:T(1024)S(1)} %bitcast.71, f32[2048,64]{1,0:T(8,128)} %copy.23, f32[]{:T(128)} %constant.14.clone.1), kind=kCustom, calls=%fused_computation.8 | custom fusion | bytes 524800 | tf_op jit(solution)/shard_map/scatter | solution.py:74
  70.7 1.1 %copy.24 = f32[64,2048]{1,0:T(8,128)} copy(f32[64,2048]{0,1:T(8,128)S(1)} %scatter_custom_fusion) | data formatting | bytes 1048576 | tf_op jit(solution)/shard_map/scatter | solution.py:74
  (7 shorter events, 0.1 us)
Async XLA Ops:
  0.0 12.6 %copy-start = (f32[8,256,256]{2,1,0:T(8,128)S(1)}, f32[8,256,256]{2,1,0:T(8,128)}, u32[]{:S(2)}) copy-start(f32[8,256,256]{2,1,0:T(8,128)} %param.14) | copy-start | bytes 6291460
  2.3 9.7 %copy-start.5 = (s32[1,2048]{1,0:T(1,128)S(1)}, s32[1,2048]{1,0:T(1,128)}, u32[]{:S(2)}) copy-start(s32[1,2048]{1,0:T(1,128)} %param.13) | copy-start | bytes 24580
  12.6 2.1 %copy-start.1 = (f32[128,2048]{1,0:T(8,128)S(1)}, f32[128,2048]{1,0:T(8,128)}, u32[]{:S(2)}) copy-start(f32[128,2048]{1,0:T(8,128)} %param.15) | copy-start | bytes 3145732
  19.6 4.6 %collective-permute-start = (f32[64,128]{1,0:T(8,128)S(1)}, f32[64,128]{1,0:T(8,128)S(1)}, u32[]{:S(2)}, u32[]{:S(2)}) collective-permute-start(f32[64,128]{1,0:T(8,128)S(1)} %psum.21), channel_id=1, source_target_pairs={{0,2},{2,0},{4,6},{6,4},{8,10},{10,8},{12,14},{14,12},{1,3},{3,1},... | collective-permute-start | bytes 98312 | tf_op jit(solution)/shard_map/ppermute | solution.py:10
  22.3 5.1 %copy-start.2 = (f32[128,2048]{1,0:T(8,128)S(1)}, f32[128,2048]{1,0:T(8,128)}, u32[]{:S(2)}) copy-start(f32[128,2048]{1,0:T(8,128)} %param.17) | copy-start | bytes 3145732
  32.1 4.0 %collective-permute-start.1 = (f32[64,128]{1,0:T(8,128)S(1)}, f32[64,128]{1,0:T(8,128)S(1)}, u32[]{:S(2)}, u32[]{:S(2)}) collective-permute-start(f32[64,128]{1,0:T(8,128)S(1)} %psum.22), channel_id=1, source_target_pairs={{0,2},{2,0},{4,6},{6,4},{8,10},{10,8},{12,14},{14,12},{1,3},{3,1},... | collective-permute-start | bytes 98312 | tf_op jit(solution)/shard_map/ppermute | solution.py:10
  36.1 4.0 %collective-permute-start.2 = (f32[64,128]{1,0:T(8,128)S(1)}, f32[64,128]{1,0:T(8,128)S(1)}, u32[]{:S(2)}, u32[]{:S(2)}) collective-permute-start(f32[64,128]{1,0:T(8,128)S(1)} %add.64), channel_id=1, source_target_pairs={{0,4},{2,6},{4,0},{6,2},{8,12},{10,14},{12,8},{14,10},{1,5},{3,7},... | collective-permute-start | bytes 98312 | tf_op jit(solution)/shard_map/ppermute | solution.py:10
  38.2 5.2 %copy-start.3 = (f32[128,2048]{1,0:T(8,128)S(1)}, f32[128,2048]{1,0:T(8,128)}, u32[]{:S(2)}) copy-start(f32[128,2048]{1,0:T(8,128)} %param.19) | copy-start | bytes 3145732
  41.4 19.4 %copy-start.4 = (f32[1,256,256]{2,1,0:T(8,128)S(1)}, f32[1,256,256]{2,1,0:T(8,128)}, u32[]{:S(2)}) copy-start(f32[1,256,256]{2,1,0:T(8,128)} %param.23) | copy-start | bytes 786436
  48.0 4.0 %collective-permute-start.3 = (f32[64,128]{1,0:T(8,128)S(1)}, f32[64,128]{1,0:T(8,128)S(1)}, u32[]{:S(2)}, u32[]{:S(2)}) collective-permute-start(f32[64,128]{1,0:T(8,128)S(1)} %psum.23), channel_id=1, source_target_pairs={{0,2},{2,0},{4,6},{6,4},{8,10},{10,8},{12,14},{14,12},{1,3},{3,1},... | collective-permute-start | bytes 98312 | tf_op jit(solution)/shard_map/ppermute | solution.py:10
  52.0 3.9 %collective-permute-start.4 = (f32[64,128]{1,0:T(8,128)S(1)}, f32[64,128]{1,0:T(8,128)S(1)}, u32[]{:S(2)}, u32[]{:S(2)}) collective-permute-start(f32[64,128]{1,0:T(8,128)S(1)} %add.67), channel_id=1, source_target_pairs={{0,4},{2,6},{4,0},{6,2},{8,12},{10,14},{12,8},{14,10},{1,5},{3,7},... | collective-permute-start | bytes 98312 | tf_op jit(solution)/shard_map/ppermute | solution.py:10
  55.9 4.9 %collective-permute-start.5 = (f32[64,128]{1,0:T(8,128)S(1)}, f32[64,128]{1,0:T(8,128)S(1)}, u32[]{:S(2)}, u32[]{:S(2)}) collective-permute-start(f32[64,128]{1,0:T(8,128)S(1)} %add.68), channel_id=1, source_target_pairs={{0,8},{2,10},{4,12},{6,14},{8,0},{10,2},{12,4},{14,6},{1,9},{3,11}... | collective-permute-start | bytes 98312 | tf_op jit(solution)/shard_map/ppermute | solution.py:10
where the time goes:
time: 72.2 us; the launch traced here: 71.8 us
  local copies, waits for them, and re-layouts  19.7 us (27%)
  matrix products  14.4 us (20%)
  starting transfers between devices  14 us (19%)
  waiting for transfers between devices  11.4 us (16%)
  blocking collectives  10.5 us (15%)
  other arithmetic  1.55 us (2%)
    ppermute x6, starting transfers between devices, partner(): lax.ppermute(shard, axis, [(i, i ^ 1 << bit) for i in range(lax.axis_size...  14 us
    ppermute x6, waiting for transfers between devices, partner(): lax.ppermute(shard, axis, [(i, i ^ 1 << bit) for i in range(lax.axis_size...  11.4 us
    psum x3, blocking collectives, apply_level(): partial_value = lax.psum(partial_value, 'inner')  10.5 us
    gather x2, local copies, waits for them, and re-layouts, on_device(): ordered = jnp.take(right_sides, local_order, axis=1)  9.12 us
    scatter x2, local copies, waits for them, and re-layouts, on_device(): return jnp.zeros_like(field).at[:, local_order].set(field)  7.32 us
    dot_general x3, matrix products, apply_level(): jnp.dot(own_half, expand_basis, precision=HIGH, preferred_element_type=jn...  5.78 us
    dot_general x3, matrix products, apply_level(): lax.dot_general(field, reduce_basis, (((1,), (1,)), ((), ())), precision=...  3.61 us
    dot_general x3, matrix products, apply_level(): lax.dot_general(stacked, node_matrix, (((1,), (1,)), ((), ())), precision...  3 us
  transfers between devices with their start and end apart: 6, of which 6 were waited for; matrix products, arithmetic and copies ran while one was open for 0% of the time, Pallas kernels for 0%

commit v1 on v0

v1 whole, which is shorter than its diff:
```python
import functools

import jax
import jax.numpy as jnp
from jax import lax
from jax.experimental import pallas as pl
from jax.experimental.pallas import tpu as pltpu
from jax.sharding import PartitionSpec as P

F32 = jnp.float32
BF16 = jnp.bfloat16
LANES = 128
NODES = 4


def halves(x):
    high = x.astype(BF16)
    return high, (x - high.astype(F32)).astype(BF16)


def mxu(x, y, transposed):
    dims = (((1,), (1 if transposed else 0,)), ((), ()))
    return lax.dot_general(x, y, dims, preferred_element_type=F32)


def dot3(x, y, transposed):
    rows = x[0].shape[0]
    both = mxu(jnp.concatenate([x[0], x[1]], axis=0), y[0], transposed)
    return both[:rows] + both[rows:] + mxu(x[0], y[1], transposed)


def pick(source, index):
    rows, columns = source.shape[0], source.shape[1]
    block = index // LANES
    place = jnp.broadcast_to(index - block * LANES, (rows, LANES))
    picked = jnp.zeros((rows, LANES), F32)
    for c in range(columns // LANES):
        part = jnp.take_along_axis(source[:, c * LANES : (c + 1) * LANES], place, axis=1)
        picked = jnp.where(block == c, part, picked)
    return picked


def kernel(
    clusters,
    inners,
    rhs_hbm,
    order_hbm,
    leaf_hbm,
    rlow_hbm,
    elow_hbm,
    rmid_hbm,
    emid_hbm,
    rtop_hbm,
    etop_hbm,
    klow_hbm,
    kmid_hbm,
    ktop_hbm,
    out_ref,
    rhs,
    order,
    leaf,
    rlow,
    elow,
    rmid,
    emid,
    rtop,
    etop,
    klow,
    kmid,
    ktop,
    field,
    field_high,
    field_low,
    ordered,
    buf_a,
    buf_g,
    src_b,
    buf_b,
    buf_c,
    buf_e,
    buf_f,
    load_sem,
    leaf_sem,
    send_sem,
    recv_sem,
    node_send,
    node_recv,
):
    rhs_count, columns = rhs.shape
    leafs, size = leaf.shape[0], leaf.shape[1]
    rank = rlow.shape[0]
    cluster, inner = lax.axis_index("cluster"), lax.axis_index("inner")
    per_node = clusters // NODES
    members = per_node * inners
    rows = rhs_count // members
    node = cluster // per_node
    place = lax.rem(cluster, per_node) * inners + inner

    def device(n, q):
        return {"cluster": n * per_node + q // inners, "inner": lax.rem(q, inners)}

    barrier = pltpu.get_barrier_semaphore()
    for step in range(1, members):
        pl.semaphore_signal(
            barrier,
            inc=1,
            device_id=device(node, lax.rem(place + step, members)),
            device_id_type=pl.DeviceIdType.MESH,
        )
    for step in range(1, NODES):
        pl.semaphore_signal(
            barrier,
            inc=1,
            device_id=device(lax.rem(node + step, NODES), place),
            device_id_type=pl.DeviceIdType.MESH,
        )

    low_half = place // (members // 2)
    mid_half = lax.rem(node, 2)
    top_half = node // 2

    def load(src, dst, sem):
        copy = pltpu.make_async_copy(src, dst, sem)
        copy.start()
        return copy

    order_copy = load(order_hbm, order, load_sem.at[0])
    rhs_copy = load(rhs_hbm, rhs, load_sem.at[1])
    leaf_copies = [load(leaf_hbm.at[b], leaf.at[b], leaf_sem.at[b]) for b in range(leafs)]
    rlow_copy = load(rlow_hbm, rlow, load_sem.at[2])
    rmid_copy = load(rmid_hbm, rmid, load_sem.at[3])
    rtop_copy = load(rtop_hbm, rtop, load_sem.at[4])
    klow_copy = load(
        klow_hbm.at[node, pl.ds(pl.multiple_of(low_half * rank, rank), rank)], klow, load_sem.at[5]
    )
    elow_copy = load(elow_hbm, elow, load_sem.at[6])
    emid_copy = load(emid_hbm, emid, load_sem.at[7])
    kmid_copy = load(kmid_hbm.at[node // 2], kmid, load_sem.at[8])
    ktop_copy = load(
        ktop_hbm.at[0, pl.ds(pl.multiple_of(top_half * rank, rank), rank)], ktop, load_sem.at[9]
    )
    etop_copy = load(etop_hbm, etop, load_sem.at[10])

    def swap(kind, src_of, dst_of):
        copies = []
        for step in range(1, members):
            to = lax.rem(place + step, members)
            copies.append(
                pltpu.make_async_remote_copy(
                    src_ref=src_of(to),
                    dst_ref=dst_of(place),
                    send_sem=send_sem.at[kind, step],
                    recv_sem=recv_sem.at[kind, step],
                    device_id=device(node, to),
                    device_id_type=pl.DeviceIdType.MESH,
                )
            )
            copies[-1].start()
        return copies

    def node_swap(kind, src, dst, to):
        copy = pltpu.make_async_remote_copy(
            src_ref=src,
            dst_ref=dst,
            send_sem=node_send.at[kind],
            recv_sem=node_recv.at[kind],
            device_id=device(to, place),
            device_id_type=pl.DeviceIdType.MESH,
        )
        copy.start()
        return copy

    order_copy.wait()
    rhs_copy.wait()
    for b in range(columns // LANES):
        cols = slice(b * LANES, (b + 1) * LANES)
        ordered[:, cols] = pick(rhs[...], order[:, cols])
    for b in range(leafs):
        cols = slice(b * size, (b + 1) * size)
        leaf_copies[b].wait()
        piece = dot3(halves(ordered[:, cols]), halves(leaf[b]), True)
        field[:, cols] = piece
        field_high[:, cols], field_low[:, cols] = halves(piece)

    def coefficients(basis):
        total = jnp.zeros((rhs_count, rank), F32)
        for b in range(leafs):
            cols = slice(b * size, (b + 1) * size)
            total += dot3(
                (field_high[:, cols], field_low[:, cols]), halves(basis[:, cols]), True
            )
        return total

    rlow_copy.wait()
    coeff_low = coefficients(rlow)
    buf_a[place] = coeff_low
    pl.semaphore_wait(barrier, members - 1 + NODES - 1)
    copies_a = swap(0, lambda to: buf_a.at[place], lambda q: buf_a.at[q])

    rtop_copy.wait()
    emid_copy.wait()

    def gram(expand, reduce):
        total = jnp.zeros((rank, rank), F32)
        for b in range(leafs):
            cols = slice(b * size, (b + 1) * size)
            total += dot3(halves(expand[:, cols]), halves(reduce[:, cols]), True)
        return total

    buf_g[place] = gram(emid, rtop)
    copies_g = swap(1, lambda to: buf_g.at[place], lambda q: buf_g.at[q])
    rmid_copy.wait()
    elow_copy.wait()
    gram_mid = gram(elow, rmid)
    gram_top = gram(elow, rtop)
    coeff_mid = coefficients(rmid)
    coeff_top = coefficients(rtop)

    def total_of(buf, first, count):
        total = buf[first]
        for q in range(first + 1, first + count):
            total += buf[q]
        return total

    for copy in copies_a:
        copy.wait()
    klow_copy.wait()
    half = members // 2
    stacked = jnp.concatenate([total_of(buf_a, 0, half), total_of(buf_a, half, half)], axis=1)
    solved_low = halves(dot3(halves(stacked), halves(klow[...]), True))
    corrected = jnp.concatenate(
        [
            coeff_mid - dot3(solved_low, halves(gram_mid), False),
            coeff_top - dot3(solved_low, halves(gram_top), False),
        ],
        axis=1,
    )
    for q in range(members):
        src_b[q] = corrected[q * rows : (q + 1) * rows]
    copies_b = swap(2, lambda to: src_b.at[to], lambda q: buf_b.at[q])
    buf_b[place] = src_b[place]

    own = order[...]
    count = columns // LANES
    position = lax.broadcasted_iota(jnp.int32, (1, columns), 1)
    spots = lax.broadcasted_iota(jnp.int32, (count, columns), 0)
    hit = own // LANES == spots
    upper = jnp.where(hit, position // 16, 0).astype(F32).astype(BF16)
    lower = jnp.where(hit, lax.rem(position, 16), 0).astype(F32).astype(BF16)
    lanes = lax.broadcasted_iota(jnp.int32, (LANES, columns), 0)
    lane_hit = jnp.where(lax.rem(own, LANES) == lanes, 1.0, 0.0).astype(BF16)
    table = mxu(jnp.concatenate([upper, lower], axis=0), lane_hit, True)
    inverse = (table[:count] * 16.0 + table[count:]).astype(jnp.int32)

    for copy in copies_b:
        copy.wait()
    summed = total_of(buf_b, 0, members)
    coeff_mid_node = summed[:, :rank]
    buf_c[mid_half] = coeff_mid_node
    pair = node + 1 - 2 * mid_half
    copy_c = node_swap(0, buf_c.at[mid_half], buf_c.at[mid_half], pair)

    for b in range(leafs):
        cols = slice(b * size, (b + 1) * size)
        field[:, cols] -= dot3(solved_low, halves(elow[:, cols]), False)

    for copy in copies_g:
        copy.wait()
    kmid_copy.wait()
    gram_node = halves(total_of(buf_g, 0, members))
    kmid_half = halves(kmid[pl.ds(pl.multiple_of(mid_half * rank, rank), rank), :])
    copy_c.wait()
    stacked = jnp.concatenate([buf_c[0], buf_c[1]], axis=1)
    solved_mid = dot3(halves(stacked), kmid_half, True)
    coeff_top_node = summed[:, rank:] - dot3(halves(solved_mid), gram_node, False)
    buf_e[node] = coeff_top_node
    copies_e = [
        node_swap(step, buf_e.at[node], buf_e.at[node], lax.rem(node + step, NODES))
        for step in range(1, NODES)
    ]
    ktop_copy.wait()
    ktop_half = halves(ktop[...])
    for copy in copies_e:
        copy.wait()
    stacked = jnp.concatenate([buf_e[0] + buf_e[1], buf_e[2] + buf_e[3]], axis=1)
    solved_top = dot3(halves(stacked), ktop_half, True)
    buf_f[place] = jnp.concatenate([solved_mid, solved_top], axis=1)
    copies_f = swap(3, lambda to: buf_f.at[place], lambda q: buf_f.at[q])
    etop_copy.wait()
    for copy in copies_f:
        copy.wait()
    solved = jnp.concatenate([buf_f[q] for q in range(members)], axis=0)
    solved = halves(solved)
    for b in range(leafs):
        cols = slice(b * size, (b + 1) * size)
        expand = jnp.concatenate([emid[:, cols], etop[:, cols]], axis=0)
        field[:, cols] -= dot3(solved, halves(expand), False)
    for b in range(count):
        out_ref[:, b * LANES : (b + 1) * LANES] = pick(field[...], inverse[b : b + 1])


def on_device(
    right_sides,
    tree_order,
    leaf_inverse,
    reduce_low,
    expand_low,
    reduce_mid,
    expand_mid,
    reduce_top,
    expand_top,
    coupling_low,
    coupling_mid,
    coupling_top,
):
    rhs_count, columns = right_sides.shape
    rank = reduce_low.shape[0]
    clusters, inners = lax.axis_size("cluster"), lax.axis_size("inner")
    members = clusters // NODES * inners
    rows = rhs_count // members
    basis = pltpu.VMEM((rank, columns), F32)
    steps = max(members, NODES)
    scratch = [
        pltpu.VMEM((rhs_count, columns), F32),
        pltpu.VMEM((1, columns), jnp.int32),
        pltpu.VMEM(leaf_inverse.shape, F32),
        basis,
        basis,
        basis,
        basis,
        basis,
        basis,
        pltpu.VMEM((rank, 2 * rank), F32),
        pltpu.VMEM((2 * rank, 2 * rank), F32),
        pltpu.VMEM((rank, 2 * rank), F32),
        pltpu.VMEM((rhs_count, columns), F32),
        pltpu.VMEM((rhs_count, columns), BF16),
        pltpu.VMEM((rhs_count, columns), BF16),
        pltpu.VMEM((rhs_count, columns), F32),
        pltpu.VMEM((members, rhs_count, rank), F32),
        pltpu.VMEM((members, rank, rank), F32),
        pltpu.VMEM((members, rows, 2 * rank), F32),
        pltpu.VMEM((members, rows, 2 * rank), F32),
        pltpu.VMEM((2, rows, rank), F32),
        pltpu.VMEM((NODES, rows, rank), F32),
        pltpu.VMEM((members, rows, 2 * rank), F32),
        pltpu.SemaphoreType.DMA((11,)),
        pltpu.SemaphoreType.DMA((leaf_inverse.shape[0],)),
        pltpu.SemaphoreType.DMA((4, steps)),
        pltpu.SemaphoreType.DMA((4, steps)),
        pltpu.SemaphoreType.DMA((NODES,)),
        pltpu.SemaphoreType.DMA((NODES,)),
    ]
    return pl.pallas_call(
        functools.partial(kernel, clusters, inners),
        out_shape=jax.ShapeDtypeStruct((rhs_count, columns), F32),
        in_specs=[pl.BlockSpec(memory_space=pl.ANY)] * 12,
        out_specs=pl.BlockSpec(memory_space=pltpu.VMEM),
        scratch_shapes=scratch,
        compiler_params=pltpu.CompilerParams(
            collective_id=0, has_side_effects=True, vmem_limit_bytes=50 * 1024 * 1024
        ),
    )(
        right_sides,
        tree_order,
        leaf_inverse,
        reduce_low,
        expand_low,
        reduce_mid,
        expand_mid,
        reduce_top,
        expand_top,
        coupling_low,
        coupling_mid,
        coupling_top,
    )


def solution(mesh):
    in_specs = (
        P(None, ("groups", "cluster", "inner")),
        P(("cluster", "inner"), None),
        P(("cluster", "inner"), None, None),
        P(None, ("cluster", "inner")),
        P(None, ("cluster", "inner")),
        P(None, ("cluster", "inner")),
        P(None, ("cluster", "inner")),
        P(None, ("cluster", "inner")),
        P(None, ("cluster", "inner")),
        P(),
        P(),
        P(),
    )
    out_specs = P(None, ("groups", "cluster", "inner"))
    return jax.shard_map(
        on_device, mesh=mesh, in_specs=in_specs, out_specs=out_specs, check_vma=False
    )
```

time: 72.2 us -> 35.3 us (0.49)
  Pallas kernels: 0 us -> 28 us
  matrix products: 14.4 us -> 0 us
  starting transfers between devices: 14 us -> 0 us
  local copies, waits for them, and re-layouts: 19.7 us -> 6.97 us
  waiting for transfers between devices: 11.4 us -> 0 us
  blocking collectives: 10.5 us -> 0 us
  other arithmetic: 1.55 us -> 0 us
    pallas_call x0 -> x1, Pallas kernels: none -> 28 us  [on_device(): pl.pallas_call(functools.partial(kernel, clusters, inners), out_shape=jax...]
    dot_general x10 -> x0, matrix products: 14.4 us -> none  [the longest x3 5.78 us: apply_level(): jnp.dot(own_half, expand_basis, precision=HIGH, preferred_element_type=jn...]
    ppermute x6 -> x0, starting transfers between devices: 14 us -> none  [partner(): lax.ppermute(shard, axis, [(i, i ^ 1 << bit) for i in range(lax.axis_size...]
    ppermute x6 -> x0, waiting for transfers between devices: 11.4 us -> none  [partner(): lax.ppermute(shard, axis, [(i, i ^ 1 << bit) for i in range(lax.axis_size...]
    psum x3 -> x0, blocking collectives: 10.5 us -> none  [apply_level(): partial_value = lax.psum(partial_value, 'inner')]
    gather x2 -> x0, local copies, waits for them, and re-layouts: 9.12 us -> none  [on_device(): ordered = jnp.take(right_sides, local_order, axis=1)]
    scatter x2 -> x0, local copies, waits for them, and re-layouts: 7.32 us -> none  [on_device(): return jnp.zeros_like(field).at[:, local_order].set(field)]
    unnamed x14 -> x13, local copies, waits for them, and re-layouts: 1.91 us -> 6.97 us
  transfers between devices with their start and end apart: 6 -> 0, of which waited for: 6 -> 0; matrix products, arithmetic and copies ran while one was open for 0% -> 0% of each run, Pallas kernels for 0% -> 0%
where the time goes in v1:
time: 35.3 us; the launch traced here: 35 us
  Pallas kernels  28 us (79%)
  local copies, waits for them, and re-layouts  6.97 us (20%)
    pallas_call x1, Pallas kernels, on_device(): pl.pallas_call(functools.partial(kernel, clusters, inners), out_shape=jax...  28 us
    unnamed x13, local copies, waits for them, and re-layouts  6.97 us

profile of v1, /device:TPU:0, one launch (start us, length us, event | category | flops | bytes accessed | tf_op | source)
XLA Modules:
  0.0 35.0 jit_solution(13719145339351153392)
XLA Ops:
  0.0 0.0 copy-start
  0.0 1.2 %copy-done = f32[128,2048]{1,0:T(8,128)S(1)} copy-done((f32[128,2048]{1,0:T(8,128)S(1)}, f32[128,2048]{1,0:T(8,128)}, u32[]{:S(2)}) %copy-start) | copy-done | bytes 1048600
  1.2 0.0 copy-start.1
  1.2 1.2 %copy-done.1 = f32[128,2048]{1,0:T(8,128)S(1)} copy-done((f32[128,2048]{1,0:T(8,128)S(1)}, f32[128,2048]{1,0:T(8,128)}, u32[]{:S(2)}) %copy-start.1) | copy-done | bytes 1048600
  2.5 0.0 copy-start.2
  2.5 1.0 %copy-done.2 = f32[64,2048]{1,0:T(8,128)S(1)} copy-done((f32[64,2048]{1,0:T(8,128)S(1)}, f32[64,2048]{1,0:T(8,128)}, u32[]{:S(2)}) %copy-start.2) | copy-done | bytes 524312
  3.5 0.0 copy-start.3
  3.5 1.0 %copy-done.3 = f32[2,256,256]{2,1,0:T(8,128)S(1)} copy-done((f32[2,256,256]{2,1,0:T(8,128)S(1)}, f32[2,256,256]{2,1,0:T(8,128)}, u32[]{:S(2)}) %copy-start.3) | copy-done | bytes 524312
  4.5 0.0 copy-start.4
  4.5 0.9 %copy-done.4 = f32[1,256,256]{2,1,0:T(8,128)S(1)} copy-done((f32[1,256,256]{2,1,0:T(8,128)S(1)}, f32[1,256,256]{2,1,0:T(8,128)}, u32[]{:S(2)}) %copy-start.4) | copy-done | bytes 262168
  5.5 0.0 copy-start.5
  5.5 0.7 %copy-done.5 = s32[1,2048]{1,0:T(1,128)S(1)} copy-done((s32[1,2048]{1,0:T(1,128)S(1)}, s32[1,2048]{1,0:T(1,128)}, u32[]{:S(2)}) %copy-start.5) | copy-done | bytes 8216
  6.2 28.0 %shard_map.118 = f32[64,2048]{1,0:T(8,128)S(1)} custom-call(f32[64,2048]{1,0:T(8,128)S(1)} %copy-done.2, s32[1,2048]{1,0:T(1,128)S(1)} %copy-done.5, f32[8,256,256]{2,1,0:T(8,128)} %leaf_hbm.1, f32[128,2048]{1,0:T(8,128)S(1)} %copy-done, f32[128,2048]{1,0:T(8,128)S(1)} %copy-done.1, f32[128,2048]{1,0:T(8,128)} %rmid_hbm.1, f32[128,2048]{1,0:T(8,128)} %emid_hbm.1, ...), custom_call_target="tpu_custom_call" | custom-call | tf_op jit(solution)/shard_map/pallas_call | solution.py:354
  34.2 0.8 %copy.14 = f32[64,2048]{1,0:T(8,128)} copy(f32[64,2048]{1,0:T(8,128)S(1)} %shard_map.118) | data formatting | bytes 1048576
Async XLA Ops:
  0.0 1.2 %copy-start = (f32[128,2048]{1,0:T(8,128)S(1)}, f32[128,2048]{1,0:T(8,128)}, u32[]{:S(2)}) copy-start(f32[128,2048]{1,0:T(8,128)} %rlow_hbm.1) | copy-start | bytes 3145732
  1.2 1.2 %copy-start.1 = (f32[128,2048]{1,0:T(8,128)S(1)}, f32[128,2048]{1,0:T(8,128)}, u32[]{:S(2)}) copy-start(f32[128,2048]{1,0:T(8,128)} %elow_hbm.1) | copy-start | bytes 3145732
  2.5 1.0 %copy-start.2 = (f32[64,2048]{1,0:T(8,128)S(1)}, f32[64,2048]{1,0:T(8,128)}, u32[]{:S(2)}) copy-start(f32[64,2048]{1,0:T(8,128)} %rhs_hbm.1) | copy-start | bytes 1572868
  3.5 1.0 %copy-start.3 = (f32[2,256,256]{2,1,0:T(8,128)S(1)}, f32[2,256,256]{2,1,0:T(8,128)}, u32[]{:S(2)}) copy-start(f32[2,256,256]{2,1,0:T(8,128)} %kmid_hbm.1) | copy-start | bytes 1572868
  4.5 0.9 %copy-start.4 = (f32[1,256,256]{2,1,0:T(8,128)S(1)}, f32[1,256,256]{2,1,0:T(8,128)}, u32[]{:S(2)}) copy-start(f32[1,256,256]{2,1,0:T(8,128)} %ktop_hbm.1) | copy-start | bytes 786436
  5.5 0.7 %copy-start.5 = (s32[1,2048]{1,0:T(1,128)S(1)}, s32[1,2048]{1,0:T(1,128)}, u32[]{:S(2)}) copy-start(s32[1,2048]{1,0:T(1,128)} %order_hbm.1) | copy-start | bytes 24580

commit v2 on v1

v2 whole, which is shorter than its diff:
```python
import functools

import jax
import jax.numpy as jnp
from jax import lax
from jax.experimental import pallas as pl
from jax.experimental.pallas import tpu as pltpu
from jax.sharding import PartitionSpec as P

F32 = jnp.float32
BF16 = jnp.bfloat16
LANES = 128
NODES = 4


def halves(x):
    high = x.astype(BF16)
    return high, (x - high.astype(F32)).astype(BF16)


def mxu(x, y, transposed):
    dims = (((1,), (1 if transposed else 0,)), ((), ()))
    return lax.dot_general(x, y, dims, preferred_element_type=F32)


def dot3(x, y, transposed):
    rows = x[0].shape[0]
    both = mxu(jnp.concatenate([x[0], x[1]], axis=0), y[0], transposed)
    return both[:rows] + both[rows:] + mxu(x[0], y[1], transposed)


def pick(source, index):
    rows, columns = source.shape[0], source.shape[1]
    block = index // LANES
    place = jnp.broadcast_to(index - block * LANES, (rows, LANES))
    picked = jnp.zeros((rows, LANES), F32)
    for c in range(columns // LANES):
        part = jnp.take_along_axis(source[:, c * LANES : (c + 1) * LANES], place, axis=1)
        picked = jnp.where(block == c, part, picked)
    return picked


def kernel(
    clusters,
    inners,
    rhs_hbm,
    order_hbm,
    leaf_hbm,
    rlow_hbm,
    elow_hbm,
    rmid_hbm,
    emid_hbm,
    rtop_hbm,
    etop_hbm,
    klow_hbm,
    kmid_hbm,
    ktop_hbm,
    out_ref,
    rhs,
    order,
    leaf,
    rlow,
    elow,
    rmid,
    emid,
    rtop,
    etop,
    klow,
    kmid,
    ktop,
    field,
    field_high,
    field_low,
    ordered,
    mine,
    buf_rows,
    src_low,
    buf_low,
    src_child,
    buf_child,
    buf_pair,
    src_top,
    buf_top,
    buf_nodes,
    buf_all,
    buf_mid,
    all_mid,
    buf_last,
    load_sem,
    leaf_sem,
    send_sem,
    recv_sem,
    node_send,
    node_recv,
):
    rhs_count, columns = rhs.shape
    leafs, size = leaf.shape[0], leaf.shape[1]
    rank = rlow.shape[0]
    cluster, inner = lax.axis_index("cluster"), lax.axis_index("inner")
    per_node = clusters // NODES
    members = per_node * inners
    rows = rhs_count // members
    node = cluster // per_node
    place = lax.rem(cluster, per_node) * inners + inner

    def device(n, q):
        return {"cluster": n * per_node + q // inners, "inner": lax.rem(q, inners)}

    barrier = pltpu.get_barrier_semaphore()
    for step in range(1, members):
        pl.semaphore_signal(
            barrier,
            inc=1,
            device_id=device(node, lax.rem(place + step, members)),
            device_id_type=pl.DeviceIdType.MESH,
        )
    for step in range(1, NODES):
        pl.semaphore_signal(
            barrier,
            inc=1,
            device_id=device(lax.rem(node + step, NODES), place),
            device_id_type=pl.DeviceIdType.MESH,
        )

    low_half = place // (members // 2)
    top_half = node // 2

    def load(src, dst, sem):
        copy = pltpu.make_async_copy(src, dst, sem)
        copy.start()
        return copy

    elow_copy = load(elow_hbm, elow, load_sem.at[0])
    rmid_copy = load(rmid_hbm, rmid, load_sem.at[1])
    rtop_copy = load(rtop_hbm, rtop, load_sem.at[2])
    order_copy = load(order_hbm, order, load_sem.at[3])
    rhs_copy = load(rhs_hbm, rhs, load_sem.at[4])
    emid_copy = load(emid_hbm, emid, load_sem.at[5])
    leaf_copies = [load(leaf_hbm.at[b], leaf.at[b], leaf_sem.at[b]) for b in range(leafs)]
    rlow_copy = load(rlow_hbm, rlow, load_sem.at[6])
    klow_copy = load(klow_hbm.at[node], klow, load_sem.at[7])
    kmid_copy = load(kmid_hbm, kmid, load_sem.at[8])
    ktop_copy = load(
        ktop_hbm.at[0, pl.ds(pl.multiple_of(top_half * rank, rank), rank)], ktop, load_sem.at[9]
    )
    etop_copy = load(etop_hbm, etop, load_sem.at[10])

    def swap(kind, src_of, dst, first, size):
        copies = []
        for step in range(1, size):
            to = first + lax.rem(place - first + step, size)
            copies.append(
                pltpu.make_async_remote_copy(
                    src_ref=src_of(to),
                    dst_ref=dst,
                    send_sem=send_sem.at[kind, step],
                    recv_sem=recv_sem.at[kind, step],
                    device_id=device(node, to),
                    device_id_type=pl.DeviceIdType.MESH,
                )
            )
            copies[-1].start()
        return copies

    def node_swap(kind, ref):
        copies = []
        for step in range(1, NODES):
            copies.append(
                pltpu.make_async_remote_copy(
                    src_ref=ref,
                    dst_ref=ref,
                    send_sem=node_send.at[kind, step],
                    recv_sem=node_recv.at[kind, step],
                    device_id=device(lax.rem(node + step, NODES), place),
                    device_id_type=pl.DeviceIdType.MESH,
                )
            )
            copies[-1].start()
        return copies

    def finish(copies):
        for copy in copies:
            copy.wait()

    def total_of(buf, first, count):
        total = buf[first]
        for q in range(first + 1, first + count):
            total += buf[q]
        return total

    def gram(expand, reduce):
        total = jnp.zeros((rank, rank), F32)
        for b in range(leafs):
            cols = slice(b * size, (b + 1) * size)
            total += dot3(halves(expand[:, cols]), halves(reduce[:, cols]), True)
        return total

    half = members // 2
    base = low_half * half
    part = rank // half
    slab = rank // members

    elow_copy.wait()
    rmid_copy.wait()
    rtop_copy.wait()
    grams = jnp.concatenate([gram(elow, rmid), gram(elow, rtop)], axis=1)
    for j in range(half):
        src_child[j] = grams[j * part : (j + 1) * part]
    pl.semaphore_wait(barrier, members - 1 + NODES - 1)
    copies_child = swap(
        0, lambda to: src_child.at[to - base], buf_child.at[place - base], base, half
    )
    buf_child[place - base] = src_child[place - base]
    emid_copy.wait()
    gram_node = gram(emid, rtop)
    for q in range(members):
        src_top[q] = gram_node[q * slab : (q + 1) * slab]
    copies_top = swap(1, lambda to: src_top.at[to], buf_top.at[place], 0, members)
    buf_top[place] = src_top[place]

    order_copy.wait()
    rhs_copy.wait()
    blocks = columns // LANES
    for b in range(blocks):
        cols = slice(b * LANES, (b + 1) * LANES)
        ordered[:, cols] = pick(rhs[...], order[:, cols])
        if b == blocks // 2:
            finish(copies_child)
            buf_pair[place] = total_of(buf_child, 0, half)
            copies_pair = swap(2, lambda to: buf_pair.at[place], buf_pair.at[place], 0, members)
    finish(copies_top)
    buf_nodes[node] = total_of(buf_top, 0, members)
    copies_nodes = node_swap(0, buf_nodes.at[node])
    for b in range(leafs):
        cols = slice(b * size, (b + 1) * size)
        leaf_copies[b].wait()
        piece = dot3(halves(ordered[:, cols]), halves(leaf[b]), True)
        field[:, cols] = piece
        field_high[:, cols], field_low[:, cols] = halves(piece)

    def coefficients(basis):
        total = jnp.zeros((rhs_count, rank), F32)
        for b in range(leafs):
            cols = slice(b * size, (b + 1) * size)
            total += dot3(
                (field_high[:, cols], field_low[:, cols]), halves(basis[:, cols]), True
            )
        return total

    rlow_copy.wait()
    for k, basis in enumerate((rlow, rmid, rtop)):
        coeff = coefficients(basis)
        for q in range(members):
            mine[q, :, k * rank : (k + 1) * rank] = coeff[q * rows : (q + 1) * rows]
    copies_rows = swap(3, lambda to: mine.at[to], buf_rows.at[place], 0, members)
    buf_rows[place] = mine[place]
    finish(copies_nodes)
    copies_all = swap(4, lambda to: buf_nodes, buf_all.at[place], 0, members)
    buf_all[place] = buf_nodes[...]

    klow_copy.wait()
    klow_parts = halves(klow[...])
    finish(copies_pair)
    pair_parts = halves(jnp.concatenate([buf_pair[q] for q in range(members)], axis=0))
    finish(copies_rows)
    first, second = total_of(buf_rows, 0, half), total_of(buf_rows, half, half)
    stacked = jnp.concatenate([first[:, :rank], second[:, :rank]], axis=1)
    solved = dot3(halves(stacked), klow_parts, True)
    later = first[:, rank:] + second[:, rank:]
    buf_mid[node] = later - dot3(halves(solved), pair_parts, False)
    copies_mid = node_swap(1, buf_mid.at[node])
    src_low[0] = solved[:, :rank]
    src_low[1] = solved[:, rank:]
    copies_low = swap(5, lambda to: src_low.at[to // half], buf_low.at[place], 0, members)
    buf_low[place] = src_low[low_half]

    own = order[...]
    count = columns // LANES
    position = lax.broadcasted_iota(jnp.int32, (1, columns), 1)
    spots = lax.broadcasted_iota(jnp.int32, (count, columns), 0)
    hit = own // LANES == spots
    upper = jnp.where(hit, position // 16, 0).astype(F32).astype(BF16)
    lower = jnp.where(hit, lax.rem(position, 16), 0).astype(F32).astype(BF16)
    lanes = lax.broadcasted_iota(jnp.int32, (LANES, columns), 0)
    lane_hit = jnp.where(lax.rem(own, LANES) == lanes, 1.0, 0.0).astype(BF16)
    table = mxu(jnp.concatenate([upper, lower], axis=0), lane_hit, True)
    inverse = (table[:count] * 16.0 + table[count:]).astype(jnp.int32)

    kmid_copy.wait()
    ktop_copy.wait()
    kmid_parts = [halves(kmid[n]) for n in range(NODES // 2)]
    ktop_parts = halves(ktop[...])
    finish(copies_low)
    solved_low = halves(jnp.concatenate([buf_low[q] for q in range(members)], axis=0))
    for b in range(leafs):
        cols = slice(b * size, (b + 1) * size)
        field[:, cols] -= dot3(solved_low, halves(elow[:, cols]), False)
    finish(copies_all)
    all_parts = [
        halves(
            jnp.concatenate(
                [buf_all[q, 2 * n + k] for k in range(2) for q in range(members)], axis=0
            )
        )
        for n in range(NODES // 2)
    ]
    finish(copies_mid)
    tops = []
    for n in range(NODES // 2):
        left, right = buf_mid[2 * n], buf_mid[2 * n + 1]
        stacked = jnp.concatenate([left[:, :rank], right[:, :rank]], axis=1)
        solved = dot3(halves(stacked), kmid_parts[n], True)
        all_mid[2 * n] = solved[:, :rank]
        all_mid[2 * n + 1] = solved[:, rank:]
        later = left[:, rank:] + right[:, rank:]
        tops.append(later - dot3(halves(solved), all_parts[n], False))
    solved_top = dot3(halves(jnp.concatenate(tops, axis=1)), ktop_parts, True)
    buf_last[place] = jnp.concatenate([all_mid[node], solved_top], axis=1)
    copies_last = swap(6, lambda to: buf_last.at[place], buf_last.at[place], 0, members)
    etop_copy.wait()
    finish(copies_last)
    solved = jnp.concatenate([buf_last[q] for q in range(members)], axis=0)
    solved = halves(solved)
    for b in range(leafs):
        cols = slice(b * size, (b + 1) * size)
        expand = jnp.concatenate([emid[:, cols], etop[:, cols]], axis=0)
        field[:, cols] -= dot3(solved, halves(expand), False)
    for b in range(count):
        out_ref[:, b * LANES : (b + 1) * LANES] = pick(field[...], inverse[b : b + 1])


def on_device(
    right_sides,
    tree_order,
    leaf_inverse,
    reduce_low,
    expand_low,
    reduce_mid,
    expand_mid,
    reduce_top,
    expand_top,
    coupling_low,
    coupling_mid,
    coupling_top,
):
    rhs_count, columns = right_sides.shape
    rank = reduce_low.shape[0]
    clusters, inners = lax.axis_size("cluster"), lax.axis_size("inner")
    members = clusters // NODES * inners
    rows = rhs_count // members
    basis = pltpu.VMEM((rank, columns), F32)
    half = members // 2
    slab = rank // members
    scratch = [
        pltpu.VMEM((rhs_count, columns), F32),
        pltpu.VMEM((1, columns), jnp.int32),
        pltpu.VMEM(leaf_inverse.shape, F32),
        basis,
        basis,
        basis,
        basis,
        basis,
        basis,
        pltpu.VMEM((2 * rank, 2 * rank), F32),
        pltpu.VMEM((NODES // 2, 2 * rank, 2 * rank), F32),
        pltpu.VMEM((rank, 2 * rank), F32),
        pltpu.VMEM((rhs_count, columns), F32),
        pltpu.VMEM((rhs_count, columns), BF16),
        pltpu.VMEM((rhs_count, columns), BF16),
        pltpu.VMEM((rhs_count, columns), F32),
        pltpu.VMEM((members, rows, 3 * rank), F32),
        pltpu.VMEM((members, rows, 3 * rank), F32),
        pltpu.VMEM((2, rows, rank), F32),
        pltpu.VMEM((members, rows, rank), F32),
        pltpu.VMEM((half, rank // half, 2 * rank), F32),
        pltpu.VMEM((half, rank // half, 2 * rank), F32),
        pltpu.VMEM((members, rank // half, 2 * rank), F32),
        pltpu.VMEM((members, slab, rank), F32),
        pltpu.VMEM((members, slab, rank), F32),
        pltpu.VMEM((NODES, slab, rank), F32),
        pltpu.VMEM((members, NODES, slab, rank), F32),
        pltpu.VMEM((NODES, rows, 2 * rank), F32),
        pltpu.VMEM((NODES, rows, rank), F32),
        pltpu.VMEM((members, rows, 2 * rank), F32),
        pltpu.SemaphoreType.DMA((11,)),
        pltpu.SemaphoreType.DMA((leaf_inverse.shape[0],)),
        pltpu.SemaphoreType.DMA((7, members)),
        pltpu.SemaphoreType.DMA((7, members)),
        pltpu.SemaphoreType.DMA((2, NODES)),
        pltpu.SemaphoreType.DMA((2, NODES)),
    ]
    return pl.pallas_call(
        functools.partial(kernel, clusters, inners),
        out_shape=jax.ShapeDtypeStruct((rhs_count, columns), F32),
        in_specs=[pl.BlockSpec(memory_space=pl.ANY)] * 12,
        out_specs=pl.BlockSpec(memory_space=pltpu.VMEM),
        scratch_shapes=scratch,
        compiler_params=pltpu.CompilerParams(
            collective_id=0, has_side_effects=True, vmem_limit_bytes=63 * 1024 * 1024
        ),
    )(
        right_sides,
        tree_order,
        leaf_inverse,
        reduce_low,
        expand_low,
        reduce_mid,
        expand_mid,
        reduce_top,
        expand_top,
        coupling_low,
        coupling_mid,
        coupling_top,
    )


def solution(mesh):
    in_specs = (
        P(None, ("groups", "cluster", "inner")),
        P(("cluster", "inner"), None),
        P(("cluster", "inner"), None, None),
        P(None, ("cluster", "inner")),
        P(None, ("cluster", "inner")),
        P(None, ("cluster", "inner")),
        P(None, ("cluster", "inner")),
        P(None, ("cluster", "inner")),
        P(None, ("cluster", "inner")),
        P(),
        P(),
        P(),
    )
    out_specs = P(None, ("groups", "cluster", "inner"))
    return jax.shard_map(
        on_device, mesh=mesh, in_specs=in_specs, out_specs=out_specs, check_vma=False
    )
```

time: 35.3 us -> 30.8 us (0.87)
  local copies, waits for them, and re-layouts: 6.97 us -> 1.87 us
  Pallas kernels: 28 us -> 28.8 us
    unnamed x13 -> x1, local copies, waits for them, and re-layouts: 6.97 us -> 1.87 us
    pallas_call x1, Pallas kernels: 28 us -> 28.8 us  [on_device(): pl.pallas_call(functools.partial(kernel, clusters, inners), out_shape=jax...]
where the time goes in v2:
time: 30.8 us; the launch traced here: 30.7 us
  Pallas kernels  28.8 us (94%)
  local copies, waits for them, and re-layouts  1.87 us (6%)
    pallas_call x1, Pallas kernels, on_device(): pl.pallas_call(functools.partial(kernel, clusters, inners), out_shape=jax...  28.8 us
    unnamed x1, local copies, waits for them, and re-layouts  1.87 us

profile of v2, /device:TPU:0, one launch (start us, length us, event | category | flops | bytes accessed | tf_op | source)
XLA Modules:
  0.0 30.7 jit_solution(14603105985282907558)
XLA Ops:
  0.0 28.8 %shard_map.118 = f32[64,2048]{1,0:T(8,128)} custom-call(f32[64,2048]{1,0:T(8,128)} %rhs_hbm.1, s32[1,2048]{1,0:T(1,128)} %order_hbm.1, f32[8,256,256]{2,1,0:T(8,128)} %leaf_hbm.1, f32[128,2048]{1,0:T(8,128)} %rlow_hbm.1, f32[128,2048]{1,0:T(8,128)} %elow_hbm.1, f32[128,2048]{1,0:T(8,128)} %rmid_hbm.1, f32[128,2048]{1,0:T(8,128)} %emid_hbm.1, ...), custom_call_target="tpu_custom_call" | custom-call | tf_op jit(solution)/shard_map/pallas_call | solution.py:392
  28.8 1.9 %copy.14 = f32[64,2048]{1,0:T(8,128)} copy(f32[64,2048]{1,0:T(8,128)} %shard_map.118) | data formatting | bytes 1048576

commit v3 on v2

--- a/solution.py
+++ b/solution.py
@@ -206,16 +206,11 @@
     grams = jnp.concatenate([gram(elow, rmid), gram(elow, rtop)], axis=1)
     for j in range(half):
         src_child[j] = grams[j * part : (j + 1) * part]
-    pl.semaphore_wait(barrier, members - 1 + NODES - 1)
-    copies_child = swap(
-        0, lambda to: src_child.at[to - base], buf_child.at[place - base], base, half
-    )
     buf_child[place - base] = src_child[place - base]
     emid_copy.wait()
     gram_node = gram(emid, rtop)
     for q in range(members):
         src_top[q] = gram_node[q * slab : (q + 1) * slab]
-    copies_top = swap(1, lambda to: src_top.at[to], buf_top.at[place], 0, members)
     buf_top[place] = src_top[place]
 
     order_copy.wait()
@@ -224,19 +219,22 @@
     for b in range(blocks):
         cols = slice(b * LANES, (b + 1) * LANES)
         ordered[:, cols] = pick(rhs[...], order[:, cols])
-        if b == blocks // 2:
-            finish(copies_child)
-            buf_pair[place] = total_of(buf_child, 0, half)
-            copies_pair = swap(2, lambda to: buf_pair.at[place], buf_pair.at[place], 0, members)
-    finish(copies_top)
-    buf_nodes[node] = total_of(buf_top, 0, members)
-    copies_nodes = node_swap(0, buf_nodes.at[node])
+    pl.semaphore_wait(barrier, members - 1 + NODES - 1)
+    copies_child = swap(
+        0, lambda to: src_child.at[to - base], buf_child.at[place - base], base, half
+    )
+    copies_top = swap(1, lambda to: src_top.at[to], buf_top.at[place], 0, members)
+    for copy in leaf_copies:
+        copy.wait()
     for b in range(leafs):
         cols = slice(b * size, (b + 1) * size)
-        leaf_copies[b].wait()
         piece = dot3(halves(ordered[:, cols]), halves(leaf[b]), True)
         field[:, cols] = piece
         field_high[:, cols], field_low[:, cols] = halves(piece)
+
+    finish(copies_child)
+    buf_pair[place] = total_of(buf_child, 0, half)
+    copies_pair = swap(2, lambda to: buf_pair.at[place], buf_pair.at[place], 0, members)
 
     def coefficients(basis):
         total = jnp.zeros((rhs_count, rank), F32)
@@ -249,17 +247,18 @@
 
     rlow_copy.wait()
     for k, basis in enumerate((rlow, rmid, rtop)):
+        if k == 2:
+            finish(copies_top)
+            buf_nodes[node] = total_of(buf_top, 0, members)
+            copies_nodes = node_swap(0, buf_nodes.at[node])
         coeff = coefficients(basis)
         for q in range(members):
             mine[q, :, k * rank : (k + 1) * rank] = coeff[q * rows : (q + 1) * rows]
     copies_rows = swap(3, lambda to: mine.at[to], buf_rows.at[place], 0, members)
     buf_rows[place] = mine[place]
-    finish(copies_nodes)
-    copies_all = swap(4, lambda to: buf_nodes, buf_all.at[place], 0, members)
-    buf_all[place] = buf_nodes[...]
-
     klow_copy.wait()
     klow_parts = halves(klow[...])
+
     finish(copies_pair)
     pair_parts = halves(jnp.concatenate([buf_pair[q] for q in range(members)], axis=0))
     finish(copies_rows)
@@ -273,6 +272,9 @@
     src_low[1] = solved[:, rank:]
     copies_low = swap(5, lambda to: src_low.at[to // half], buf_low.at[place], 0, members)
     buf_low[place] = src_low[low_half]
+    finish(copies_nodes)
+    copies_all = swap(4, lambda to: buf_nodes, buf_all.at[place], 0, members)
+    buf_all[place] = buf_nodes[...]
 
     own = order[...]
     count = columns // LANES

time: 30.8 us -> 30 us (0.974)
  Pallas kernels: 28.8 us -> 27.9 us
    pallas_call x1, Pallas kernels: 28.8 us -> 27.9 us  [on_device(): pl.pallas_call(functools.partial(kernel, clusters, inners), out_shape=jax...]
where the time goes in v3:
time: 30 us; the launch traced here: 29.8 us
  Pallas kernels  27.9 us (93%)
  local copies, waits for them, and re-layouts  1.87 us (6%)
    pallas_call x1, Pallas kernels, on_device(): pl.pallas_call(functools.partial(kernel, clusters, inners), out_shape=jax...  27.9 us
    unnamed x1, local copies, waits for them, and re-layouts  1.87 us

profile of v3, /device:TPU:0, one launch (start us, length us, event | category | flops | bytes accessed | tf_op | source)
XLA Modules:
  0.0 29.8 jit_solution(5729819731072582747)
XLA Ops:
  0.0 27.9 %shard_map.118 = f32[64,2048]{1,0:T(8,128)} custom-call(f32[64,2048]{1,0:T(8,128)} %rhs_hbm.1, s32[1,2048]{1,0:T(1,128)} %order_hbm.1, f32[8,256,256]{2,1,0:T(8,128)} %leaf_hbm.1, f32[128,2048]{1,0:T(8,128)} %rlow_hbm.1, f32[128,2048]{1,0:T(8,128)} %elow_hbm.1, f32[128,2048]{1,0:T(8,128)} %rmid_hbm.1, f32[128,2048]{1,0:T(8,128)} %emid_hbm.1, ...), custom_call_target="tpu_custom_call" | custom-call | tf_op jit(solution)/shard_map/pallas_call | solution.py:394
  27.9 1.9 %copy.14 = f32[64,2048]{1,0:T(8,128)} copy(f32[64,2048]{1,0:T(8,128)} %shard_map.118) | data formatting | bytes 1048576
